TPU v7x, 128 devices: a whole 4x4x4 slice. The times are simulated.
128 devices in a mesh: grp: 4 (over x), fsdp: 32 (over y, z, core).
Axes of the slice: x: 4, y: 4, z: 4, core: 2. Of those that a mesh axis runs over, the one named last changes fastest.
Arguments:
- tokens: bfloat16 [8192, 4096], P('fsdp'), may hold values from -550 to 550
- attn_gain: float32 [4096], replicated, may hold values from 0.1 to 1.9
- ffn_gain: float32 [4096], replicated, may hold values from 0.1 to 1.9
- w_query: bfloat16 [4096, 4096], P('fsdp', 'grp'), may hold values from -2.421875 to 2.421875
- w_key: bfloat16 [4096, 256], P('fsdp'), may hold values from -0.078125 to 0.078125
- value_weight: bfloat16 [4096, 256], P('fsdp'), may hold values from -0.09375 to 0.09375
- w_out: bfloat16 [4096, 4096], P('grp', 'fsdp'), may hold values from -0.5 to 0.5
- routes: int32 [8192, 8], P('fsdp'), may hold values from 0 to 127, all different within a row; in each aligned block of 256 rows (0 to 255, 256 to 511, ...) at most 24 rows name the same one
- route_probs: bfloat16 [8192, 8], P('fsdp'), may hold values from 0.049804688 to 0.3984375
- w_gate_up: bfloat16 [128, 4096, 1536], P(('grp', 'fsdp')), may hold values from -0.09375 to 0.09375
- w_down: bfloat16 [128, 768, 4096], P(('grp', 'fsdp')), may hold values from -0.21875 to 0.21875
Outputs:
- attn_branch: bfloat16 [8192, 4096], P('fsdp')
- layer_out: bfloat16 [8192, 4096], P('fsdp', 'grp')
Inputs may be any that keep to these rules, and one draw needn't show every extreme that they name: `routes`: each row names 8 different experts. Among the 256 rows of one device (aligned blocks), no expert is named more than 24 times, a bound that some block reaches.
All inputs are finite; a program needn't handle non-finite values.
Results may differ from a plain program's by a relative error of at most 0.015.
Values may be sent and summed in bfloat16 or wider, within the bound.
No kernel may reach another device: no remote copies, remote signals or barrier semaphores. Data moves between devices by JAX's collectives and lax.ppermute only.
A program may use at most 128 MiB of HBM per device.

v0:
```python
import jax
import jax.numpy as jnp
from jax import lax
from jax.sharding import PartitionSpec as P

KEY_VALUE_HEADS = 2
HEAD_DIMENSION = 128
FFW = 768
EPSILON = 1e-06
FLOOR_SCORE = -1e30


def rms_scale(row_data, gain):
    floats = row_data.astype(jnp.float32)
    mean_sq = jnp.mean(floats * floats, axis=-1, keepdims=True)
    return (floats * lax.rsqrt(mean_sq + EPSILON) * gain).astype(jnp.bfloat16)


def attend_block(state, query_bf, key_block, value_block, key_start, positions):
    row_best, row_total, weighted = state
    scores = jnp.einsum(
        "thd,kd->thk", query_bf, key_block, preferred_element_type=jnp.float32
    ) * HEAD_DIMENSION ** (-0.5)
    key_pos = key_start + jnp.arange(key_block.shape[0], dtype=jnp.int32)
    allowed = (key_pos[None, :] <= positions[:, None])[:, None, :]
    masked = jnp.where(allowed, scores, FLOOR_SCORE)
    new_best = jnp.maximum(row_best, jnp.max(masked, axis=2))
    weights = jnp.where(allowed, jnp.exp(masked - new_best[:, :, None]), 0.0)
    rescale = jnp.exp(row_best - new_best)
    row_total = row_total * rescale + jnp.sum(weights, axis=2)
    weighted = weighted * rescale[:, :, None] + jnp.einsum(
        "thk,kd->thd", weights.astype(jnp.bfloat16), value_block, preferred_element_type=jnp.float32
    )
    return (new_best, row_total, weighted)


def on_device(
    tokens,
    attn_gain,
    ffn_gain,
    w_query,
    w_key,
    value_weight,
    w_out,
    routes,
    route_probs,
    w_gate_up,
    w_down,
):
    head_groups = lax.axis_size("grp")
    fsdp_size = lax.axis_size("fsdp")
    current_group = lax.axis_index("grp")
    my_rank = lax.axis_index("fsdp")
    tok_rows = tokens.shape[0]
    model_width = tokens.shape[1]
    head_width = w_query.shape[1]
    group_heads = head_width // HEAD_DIMENSION
    key_value_head = current_group * KEY_VALUE_HEADS // head_groups
    normed = rms_scale(tokens, attn_gain)
    key_cols = lax.dynamic_slice_in_dim(w_key, key_value_head * HEAD_DIMENSION, HEAD_DIMENSION, 1)
    value_cols = lax.dynamic_slice_in_dim(
        value_weight, key_value_head * HEAD_DIMENSION, HEAD_DIMENSION, 1
    )
    query = jnp.dot(
        normed,
        lax.all_gather(w_query, "fsdp", axis=0, tiled=True),
        preferred_element_type=jnp.float32,
    )
    key_local = jnp.dot(
        normed,
        lax.all_gather(key_cols, "fsdp", axis=0, tiled=True),
        preferred_element_type=jnp.float32,
    )
    value_local = jnp.dot(
        normed,
        lax.all_gather(value_cols, "fsdp", axis=0, tiled=True),
        preferred_element_type=jnp.float32,
    )
    query_bf = query.astype(jnp.bfloat16).reshape(tok_rows, group_heads, HEAD_DIMENSION)
    key_local = key_local.astype(jnp.bfloat16)
    value_local = value_local.astype(jnp.bfloat16)
    first_row = my_rank * tok_rows
    positions = first_row + jnp.arange(tok_rows, dtype=jnp.int32)
    last_query = first_row + tok_rows - 1
    attend_init = (
        jnp.full((tok_rows, group_heads), FLOOR_SCORE, jnp.float32),
        jnp.zeros((tok_rows, group_heads), jnp.float32),
        jnp.zeros((tok_rows, group_heads, HEAD_DIMENSION), jnp.float32),
    )
    state = attend_init
    key_rows = lax.all_gather(key_local, "fsdp", axis=0, tiled=True)
    value_rows = lax.all_gather(value_local, "fsdp", axis=0, tiled=True)
    row_count = key_rows.shape[0]
    key_span = 1024

    def visit(running, step_index):
        block_start = step_index * key_span
        key_block = lax.dynamic_slice_in_dim(key_rows, block_start, key_span, 0)
        value_block = lax.dynamic_slice_in_dim(value_rows, block_start, key_span, 0)
        needed = block_start <= last_query
        running = lax.cond(
            needed,
            lambda inner: attend_block(
                inner, query_bf, key_block, value_block, block_start, positions
            ),
            lambda inner: inner,
            running,
        )
        return (running, None)

    state, _ = lax.scan(visit, state, jnp.arange(row_count // key_span, dtype=jnp.int32))
    row_best, row_total, weighted = state
    attended = (weighted / row_total[:, :, None]).astype(jnp.bfloat16).reshape(tok_rows, head_width)
    head_part = jnp.dot(
        attended,
        lax.all_gather(w_out, "fsdp", axis=1, tiled=True),
        preferred_element_type=jnp.float32,
    ).astype(jnp.bfloat16)
    attn_branch = lax.psum(head_part.astype(jnp.float32).astype(jnp.bfloat16), "grp")
    resid = (tokens.astype(jnp.float32) + attn_branch.astype(jnp.float32)).astype(jnp.bfloat16)
    ffn_in = rms_scale(resid, ffn_gain)
    top_count = routes.shape[1]
    experts_all = head_groups * fsdp_size
    capacity = max(2, 3 * tok_rows * top_count // (2 * experts_all))
    group_rows = fsdp_size * capacity
    group_experts = fsdp_size
    expert_ids = current_group * group_experts + jnp.arange(group_experts, dtype=jnp.int32)
    named = routes[:, :, None] == expert_ids[None, None, :]
    hits = jnp.any(named, axis=1)
    token_ids = jnp.arange(tok_rows, dtype=jnp.int32)
    earlier = (token_ids[None, :] < token_ids[:, None]).astype(jnp.bfloat16)
    rank = jnp.dot(earlier, hits.astype(jnp.bfloat16), preferred_element_type=jnp.float32)
    code = jnp.where(hits, rank, -1.0).astype(jnp.bfloat16)
    row_ids = jnp.arange(group_rows, dtype=jnp.int32)
    spread = (
        row_ids[None, :] // capacity == jnp.arange(group_experts, dtype=jnp.int32)[:, None]
    ).astype(jnp.bfloat16)
    code_rows = jnp.dot(code, spread, preferred_element_type=jnp.float32)
    slot_match = code_rows == (row_ids % capacity).astype(jnp.float32)[None, :]
    chosen = slot_match.astype(jnp.bfloat16)
    outbound = (
        jnp.einsum("tr,td->rd", chosen, ffn_in, preferred_element_type=jnp.float32)
        .astype(jnp.bfloat16)
        .reshape(fsdp_size, capacity, model_width)
    )
    gate_proj = w_gate_up[0]
    down_proj = w_down[0]
    col_width = model_width // head_groups
    arrived = lax.all_to_all(outbound, "fsdp", split_axis=0, concat_axis=0, tiled=True)
    slot_count = arrived.shape[1]
    arrived_rows = arrived.reshape(-1, model_width)
    gate_up = jnp.dot(arrived_rows, gate_proj, preferred_element_type=jnp.float32)
    hidden = (jax.nn.silu(gate_up[:, :FFW]) * gate_up[:, FFW:]).astype(jnp.bfloat16)
    result = jnp.dot(hidden, down_proj, preferred_element_type=jnp.float32).astype(jnp.bfloat16)
    returned = lax.all_to_all(
        result.reshape(fsdp_size, slot_count, model_width),
        "fsdp",
        split_axis=0,
        concat_axis=0,
        tiled=True,
    )
    named_probs = jnp.sum(jnp.where(named, route_probs[:, :, None], 0.0), axis=1)
    prob_rows = jnp.dot(
        named_probs.astype(jnp.bfloat16), spread, preferred_element_type=jnp.float32
    )
    mixing = jnp.where(slot_match, prob_rows, 0.0).astype(jnp.bfloat16)
    group_part = jnp.dot(
        mixing, returned.reshape(group_rows, model_width), preferred_element_type=jnp.float32
    ).astype(jnp.bfloat16)
    expert_mix = lax.psum_scatter(
        group_part.astype(jnp.float32).astype(jnp.bfloat16), "grp", scatter_dimension=1, tiled=True
    ).astype(jnp.float32)
    own_cols = lax.dynamic_slice_in_dim(resid, current_group * col_width, col_width, 1)
    layer_out = (own_cols.astype(jnp.float32) + expert_mix).astype(jnp.bfloat16)
    return (attn_branch, layer_out)


def solution(mesh):
    placed = (
        P("fsdp", None),
        P(),
        P(),
        P("fsdp", "grp"),
        P("fsdp", None),
        P("fsdp", None),
        P("grp", "fsdp"),
        P("fsdp", None),
        P("fsdp", None),
        P(("grp", "fsdp"), None, None),
        P(("grp", "fsdp"), None, None),
    )
    return jax.shard_map(
        on_device,
        mesh=mesh,
        in_specs=placed,
        out_specs=(P("fsdp", None), P("fsdp", "grp")),
        check_vma=False,
    )
```

profile of v0, /device:TPU:1, one launch (start us, length us, event | category | flops | bytes accessed | tf_op | source)
XLA Modules:
  0.0 637.6 jit_solution(7689715145708267044)
XLA Ops:
  7.2 0.0 copy-start
  7.2 0.0 all-gather.13.cloned.1.call-start
  7.3 0.7 copy-done
  8.0 0.6 constant_dynamic-slice_fusion
  8.6 0.0 all-gather.13.cloned.1.call-update
  8.7 0.0 all-gather.7.cloned.1.call-start
  8.7 1.4 constant_dynamic-slice_fusion.1
  10.1 0.0 all-gather.7.cloned.1.call-update
  10.1 0.0 all-gather.11.cloned.1.call-start
  10.2 0.7 all-gather.11.cloned.1.call-update
  10.8 0.0 all-gather.15.cloned.1.call-start
  10.9 2.1 fusion.27
  13.0 44.5 %all-gather.13.cloned.1.call-done = bf16[4096,128]{1,0:T(8,128)(2,1)} async-done(((bf16[128,128]{1,0:T(8,128)(2,1)}), bf16[4096,128]{1,0:T(8,128)(2,1)}) %all-gather.13.cloned.1.call-update) | async-done | bytes 1048592 | tf_op jit(solution)/shard_map/all_gather | solution.py:76
  57.5 3.3 convolution_convert_fusion.5
  60.8 0.0 all-gather.15.cloned.1.call-update
  60.8 0.0 all-gather.9.cloned.1.call-start
  60.9 41.6 %all-gather.7.cloned.1.call-done = bf16[4096,128]{1,0:T(8,128)(2,1)} async-done(((bf16[128,128]{1,0:T(8,128)(2,1)}), bf16[4096,128]{1,0:T(8,128)(2,1)}) %all-gather.7.cloned.1.call-update) | async-done | bytes 1048592 | tf_op jit(solution)/shard_map/all_gather | solution.py:71
  102.4 2.7 convolution_convert_fusion.6
  105.1 0.0 all-gather.9.cloned.1.call-update
  105.1 0.0 all-gather.17.cloned.1.call-start
  105.2 0.5 all-gather.17.cloned.1.call-update
  105.7 0.0 all-reduce.2.cloned.1.call-start
  105.8 51.2 %all-gather.11.cloned.1.call-done = bf16[4096,1024]{1,0:T(8,128)(2,1)} async-done(((bf16[128,1024]{1,0:T(8,128)(2,1)}), bf16[4096,1024]{1,0:T(8,128)(2,1)}) %all-gather.11.cloned.1.call-update) | async-done | bytes 8388624 | tf_op jit(solution)/shard_map/all_gather | solution.py:66
  157.0 5.7 fusion.36
  162.7 0.1 copy.28
  162.8 40.4 %all-gather.15.cloned.1.call-done = bf16[8192,128]{1,0:T(8,128)(2,1)} async-done(((bf16[256,128]{1,0:T(8,128)(2,1)}), bf16[8192,128]{1,0:T(8,128)(2,1)}) %all-gather.15.cloned.1.call-update) | async-done | bytes 2097168 | tf_op jit(solution)/shard_map/all_gather | solution.py:92
  203.2 45.9 %all-gather.9.cloned.1.call-done = bf16[8192,128]{1,0:T(8,128)(2,1)} async-done(((bf16[256,128]{1,0:T(8,128)(2,1)}), bf16[8192,128]{1,0:T(8,128)(2,1)}) %all-gather.9.cloned.1.call-update) | async-done | bytes 2097168 | tf_op jit(solution)/shard_map/all_gather | solution.py:91
  249.1 0.1 broadcast_in_dim.77
  249.2 19.2 %while.15 = (s32[]{:T(128)}, f32[256,8]{0,1:T(8,128)S(1)}, f32[256,8]{0,1:T(8,128)S(1)}, f32[256,8,128]{2,0,1:T(8,128)S(1)}, s32[8]{0:T(128)S(1)}, /*index=5*/s3...) while((s32[]{:T(128)}, f32[256,8]{0,1:T(8,128)S(1)}, ...), condition=%wide.region_6.7_spmd.clone, body=%wide.region_1.6_spmd.clone.sunk | while | flops 1101796608 | bytes 29503820 | solution.py:111
  249.4 0.6 dynamic_slice.49
  250.7 8.7 %conditional.3 = ((f32[256,8]{0,1:T(8,128)S(1)}, f32[256,8]{0,1:T(8,128)S(1)}, f32[256,8,128]{2,0,1:T(8,128)S(1)})) conditional(s32[]{:T(128)} %convert_element_type.172, (f32[256,8]{0,1:T(8,128)S(1)}, f32[256,8]{0,1:T(8,128)S(1)}, f32[256,8,128]{2,0,1:T(8,128)S(1)}) %tuple.52, (s32[]{:T(128)}, s32[]{:T(128)}, bf16[8192,128]{1,0:T(8,128)(2,1)}, ...), branch_computations={%region_2.2_spmd, %region_3.5_spmd} | conditional | flops 1101796608 | bytes 29502546 | solution.py:101
  250.7 0.2 broadcast_compare_fusion
  250.9 2.4 fusion.2
  253.3 2.0 fusion.4
  255.4 3.9 fusion.8
  259.4 0.6 dynamic_slice.49
  260.7 0.6 dynamic_slice.49
  262.0 0.6 dynamic_slice.49
  263.3 0.6 dynamic_slice.49
  264.6 0.6 dynamic_slice.49
  265.8 0.6 dynamic_slice.49
  267.1 0.6 dynamic_slice.49
  268.4 0.3 copy.24
  268.8 0.1 divide_convert_fusion
  268.9 41.3 %all-gather.17.cloned.1.call-done = bf16[1024,4096]{1,0:T(8,128)(2,1)} async-done(((bf16[1024,128]{1,0:T(8,128)(2,1)}), bf16[1024,4096]{1,0:T(8,128)(2,1)}) %all-gather.17.cloned.1.call-update) | async-done | bytes 8388624 | tf_op jit(solution)/shard_map/all_gather | solution.py:116
  310.1 7.1 %convolution_convert_fusion.2 = bf16[256,4096]{1,0:T(8,128)(2,1)} fusion(bf16[256,1024]{0,1:T(8,128)(2,1)S(1)} %bitcast.55, bf16[1024,4096]{1,0:T(8,128)(2,1)} %all-gather.17.cloned.1.call-done), kind=kOutput, calls=%fused_computation.34 | convolution fusion | flops 2148532224 | bytes 11010048 | tf_op jit(solution)/shard_map/dot_general | solution.py:114
  317.2 0.0 all-reduce.2.cloned.1.call-update
  317.3 0.1 compare_reduce_fusion
  317.4 0.5 convolution_compare_fusion
  317.9 76.3 %all-reduce.2.cloned.1.call-done = bf16[256,4096]{1,0:T(8,128)(2,1)} async-done(((bf16[256,4096]{1,0:T(8,128)(2,1)}), bf16[256,4096]{1,0:T(8,128)(2,1)}) %all-reduce.2.cloned.1.call-update) | async-done | bytes 2097168 | tf_op jit(solution)/shard_map/psum | solution.py:119
  394.2 3.2 fusion.24
  397.4 2.0 convolution_convert_fusion
  399.4 80.9 %all_to_all.10 = bf16[32,24,4096]{2,1,0:T(8,128)(2,1)S(1)} all-to-all(bf16[32,24,4096]{2,1,0:T(8,128)(2,1)S(1)} %bitcast.51), channel_id=1, replica_groups=mesh['grp'=4,'fsdp'=32] {'fsdp'}, dimensions={0} | all-to-all | bytes 12582912 | tf_op jit(solution)/shard_map/all_to_all | solution.py:149
  480.3 11.7 %fusion.21 = f32[768,1536]{1,0:T(8,128)} fusion(bf16[768,4096]{1,0:T(8,128)(2,1)S(1)} %bitcast.54, bf16[1,4096,1536]{2,1,0:T(8,128)(2,1)S(1)} %bitcast.57), kind=kOutput, calls=%fused_computation.24 | convolution fusion | flops 9663676416 | bytes 23592960 | tf_op jit(solution)/shard_map/dot_general | solution.py:152
  491.9 10.3 %convolution_convert_fusion.1 = bf16[768,4096]{1,0:T(8,128)(2,1)} fusion(bf16[1,768,4096]{2,1,0:T(8,128)(2,1)} %param.25, f32[768,1536]{1,0:T(8,128)} %fusion.21), kind=kOutput, calls=%fused_computation.27 | convolution fusion | flops 4838522880 | bytes 17301504 | tf_op jit(solution)/shard_map/dot_general | solution.py:154
  502.2 4.8 all-to-all-start.1
  507.0 0.0 reduce-scatter.2.cloned.1.call-start
  507.1 0.1 fusion.41
  507.2 77.7 %all-to-all-done.1 = bf16[32,24,4096]{2,1,0:T(8,128)(2,1)} async-done(((bf16[32,24,4096]{2,1,0:T(8,128)(2,1)}), bf16[32,24,4096]{2,1,0:T(8,128)(2,1)}, u32[]{:S(2)}, u32[]{:S(2)}) %all-to-all-start.1) | async-done | bytes 6291488 | tf_op jit(solution)/shard_map/all_to_all | solution.py:155
  584.9 6.1 convolution_convert_fusion.3
  590.9 0.0 reduce-scatter.2.cloned.1.call-update
  591.0 34.6 %reduce-scatter.2.cloned.1.call-done = bf16[256,1024]{1,0:T(8,128)(2,1)} async-done(((bf16[256,4096]{1,0:T(8,128)(2,1)}), bf16[256,1024]{1,0:T(8,128)(2,1)}) %reduce-scatter.2.cloned.1.call-update) | async-done | bytes 524304 | tf_op jit(solution)/shard_map/reduce_scatter | solution.py:170
  625.6 2.0 add_convert_fusion
  627.6 3.1 copy.51
  (46 shorter events, 0.2 us)
Async XLA Ops:
  7.2 0.8 copy-start
  7.2 95.3 %copy-start.2 = (bf16[256,4096]{1,0:T(8,128)(2,1)S(1)}, bf16[256,4096]{1,0:T(8,128)(2,1)}, u32[]{:S(2)}) copy-start(bf16[256,4096]{1,0:T(8,128)(2,1)} %param.15) | copy-start | bytes 6291460
  7.2 95.3 %copy-start.6 = (f32[4096]{0:T(1024)S(1)}, f32[4096]{0:T(1024)}, u32[]{:S(2)}) copy-start(f32[4096]{0:T(1024)} %param.16) | copy-start | bytes 49156
  7.2 50.3 %all-gather.13.cloned.1.call-start = ((), (), s32[]{:S(2)}) async-start(), calls=%async_computation.6 | async-start | bytes 1081344 | tf_op jit(solution)/shard_map/all_gather | solution.py:76
  8.7 93.8 %all-gather.7.cloned.1.call-start = ((), (), s32[]{:S(2)}) async-start(), calls=%async_computation.3 | async-start | bytes 1081344 | tf_op jit(solution)/shard_map/all_gather | solution.py:71
  10.1 146.8 %all-gather.11.cloned.1.call-start = ((), (), s32[]{:S(2)}) async-start(), calls=%async_computation.5 | async-start | bytes 8650752 | tf_op jit(solution)/shard_map/all_gather | solution.py:66
  10.8 192.3 %all-gather.15.cloned.1.call-start = ((), (), s32[]{:S(2)}) async-start(), calls=%async_computation.7 | async-start | bytes 2162688 | tf_op jit(solution)/shard_map/all_gather | solution.py:92
  60.8 188.3 %all-gather.9.cloned.1.call-start = ((), (), s32[]{:S(2)}) async-start(), calls=%async_computation.4 | async-start | bytes 2162688 | tf_op jit(solution)/shard_map/all_gather | solution.py:91
  105.1 205.0 %all-gather.17.cloned.1.call-start = ((), (), s32[]{:S(2)}) async-start(), calls=%async_computation.8 | async-start | bytes 8650752 | tf_op jit(solution)/shard_map/all_gather | solution.py:116
  105.7 288.5 %all-reduce.2.cloned.1.call-start = ((), (), s32[]{:S(2)}) async-start(), calls=%async_computation.9 | async-start | bytes 4194304 | tf_op jit(solution)/shard_map/psum | solution.py:119
  310.1 7.2 %copy-start.3 = (s32[256,8]{0,1:T(8,128)S(1)}, s32[256,8]{0,1:T(8,128)}, u32[]{:S(2)}) copy-start(s32[256,8]{0,1:T(8,128)} %param.22) | copy-start | bytes 24580
  317.2 80.1 %copy-start.4 = (f32[4096]{0:T(1024)S(1)}, f32[4096]{0:T(1024)}, u32[]{:S(2)}) copy-start(f32[4096]{0:T(1024)} %param.17) | copy-start | bytes 49156
  397.4 82.9 %slice-start = ((s8[12582912]{0:T(1024)(128)(4,1)}), s8[4194304]{0:T(1024)(128)(4,1)S(1)}, s32[]{:S(2)}) async-start(s8[12582912]{0:T(1024)(128)(4,1)} %bitcast.56), calls=%async_computation.11 | async-start | bytes 8388608
  397.4 82.9 %slice-start.1 = ((s8[12582912]{0:T(1024)(128)(4,1)}), s8[4194304]{0:T(1024)(128)(4,1)S(1)}, s32[]{:S(2)}) async-start(s8[12582912]{0:T(1024)(128)(4,1)} %bitcast.56), calls=%async_computation.12 | async-start | bytes 8388608
  399.4 80.9 %slice-start.2 = ((s8[12582912]{0:T(1024)(128)(4,1)}), s8[4194304]{0:T(1024)(128)(4,1)S(1)}, s32[]{:S(2)}) async-start(s8[12582912]{0:T(1024)(128)(4,1)} %bitcast.56), calls=%async_computation.13 | async-start | bytes 8388608
  502.2 4.9 copy-start.5
  502.2 82.7 %all-to-all-start.1 = ((bf16[32,24,4096]{2,1,0:T(8,128)(2,1)}), bf16[32,24,4096]{2,1,0:T(8,128)(2,1)}, u32[]{:S(2)}, u32[]{:S(2)}) async-start(bf16[32,24,4096]{2,1,0:T(8,128)(2,1)} %bitcast.53), calls=%async_computation.1 | async-start | bytes 12582912 | tf_op jit(solution)/shard_map/all_to_all | solution.py:155
  507.0 118.5 %reduce-scatter.2.cloned.1.call-start = ((), (), s32[]{:S(2)}) async-start(), calls=%async_computation.10 | async-start | bytes 2621440 | tf_op jit(solution)/shard_map/reduce_scatter | solution.py:170
  584.9 45.9 %copy-start.1 = (bf16[128,256]{1,0:T(8,128)(2,1)S(1)}, bf16[128,256]{1,0:T(8,128)(2,1)}, u32[]{:S(2)}) copy-start(bf16[128,256]{1,0:T(8,128)(2,1)} %param.20) | copy-start | bytes 196612
Sparse Core Ops, SparseCore 0:
  10.9 46.5 all-gather.12
  60.3 42.0 all-gather.6
  104.7 52.1 all-gather.10
  159.6 43.4 all-gather.14
  205.9 43.2 all-gather.8
  251.2 58.9 all-gather.16
  317.4 76.7 all-reduce.1
  591.1 34.4 reduce-scatter.1
where the time goes:
time: 639 us; the launch traced here: 638 us
  waiting for transfers between devices  455 us (71%)
  blocking collectives  80.9 us (13%)
  matrix products  55.6 us (9%)
  between operations  14.4 us (2%)
  local copies, waits for them, and re-layouts  11.1 us (2%)
  other arithmetic  9.87 us (2%)
    all_to_all x1, blocking collectives, on_device(): lax.all_to_all(outbound, 'fsdp', split_axis=0, concat_axis=0, tiled=True)  80.9 us
    all_to_all x1, waiting for transfers between devices, on_device(): lax.all_to_all(result.reshape(fsdp_size, slot_count, model_width), 'fsdp'...  77.7 us
    psum x1, waiting for transfers between devices, on_device(): lax.psum(head_part.astype(jnp.float32).astype(jnp.bfloat16), 'grp')  76.3 us
    all_gather x1, waiting for transfers between devices, on_device(): lax.all_gather(w_query, 'fsdp', axis=0, tiled=True)  51.2 us
    all_gather x1, waiting for transfers between devices, on_device(): key_rows = lax.all_gather(key_local, 'fsdp', axis=0, tiled=True)  45.9 us
    all_gather x1, waiting for transfers between devices, on_device(): lax.all_gather(value_cols, 'fsdp', axis=0, tiled=True)  44.5 us
    all_gather x1, waiting for transfers between devices, on_device(): lax.all_gather(key_cols, 'fsdp', axis=0, tiled=True)  41.6 us
    all_gather x1, waiting for transfers between devices, on_device(): lax.all_gather(w_out, 'fsdp', axis=1, tiled=True)  41.3 us
  transfers between devices with their start and end apart: 9, of which 9 were waited for; matrix products, arithmetic and copies ran while one was open for 5% of the time, Pallas kernels for 0%

commit v1 on v0

--- a/solution.py
+++ b/solution.py
@@ -116,7 +116,9 @@
         lax.all_gather(w_out, "fsdp", axis=1, tiled=True),
         preferred_element_type=jnp.float32,
     ).astype(jnp.bfloat16)
-    attn_branch = lax.psum(head_part.astype(jnp.float32).astype(jnp.bfloat16), "grp")
+    attn_branch = jnp.sum(
+        lax.all_gather(head_part.astype(jnp.float32).astype(jnp.bfloat16), "grp"), axis=0
+    )
     resid = (tokens.astype(jnp.float32) + attn_branch.astype(jnp.float32)).astype(jnp.bfloat16)
     ffn_in = rms_scale(resid, ffn_gain)
     top_count = routes.shape[1]

time: 639 us -> 668 us (1.045)
  waiting for transfers between devices: 455 us -> 480 us
  other arithmetic: 9.87 us -> 16.8 us
    all_gather x0 -> x1, waiting for transfers between devices: none -> 101 us  [on_device(): lax.all_gather(head_part.astype(jnp.float32).astype(jnp.bfloat16), 'grp')]
    psum x1 -> x0, waiting for transfers between devices: 76.3 us -> none  [on_device(): lax.psum(head_part.astype(jnp.float32).astype(jnp.bfloat16), 'grp')]
    reduce_sum x0 -> x1, other arithmetic: none -> 6.89 us  [on_device(): jnp.sum(lax.all_gather(head_part.astype(jnp.float32).astype(jnp.bfloat16)...]
  transfers between devices with their start and end apart: 9 -> 9, of which waited for: 9 -> 9; matrix products, arithmetic and copies ran while one was open for 5% -> 4% of each run, Pallas kernels for 0% -> 0%
where the time goes in v1:
time: 668 us; the launch traced here: 667 us
  waiting for transfers between devices  480 us (72%)
  blocking collectives  80.9 us (12%)
  matrix products  55.8 us (8%)
  other arithmetic  16.8 us (3%)
  between operations  14.4 us (2%)
  local copies, waits for them, and re-layouts  8.01 us (1%)
    all_gather x1, waiting for transfers between devices, on_device(): lax.all_gather(head_part.astype(jnp.float32).astype(jnp.bfloat16), 'grp')  101 us
    all_to_all x1, blocking collectives, on_device(): lax.all_to_all(outbound, 'fsdp', split_axis=0, concat_axis=0, tiled=True)  80.9 us
    all_to_all x1, waiting for transfers between devices, on_device(): lax.all_to_all(result.reshape(fsdp_size, slot_count, model_width), 'fsdp'...  77.7 us
    all_gather x1, waiting for transfers between devices, on_device(): lax.all_gather(w_query, 'fsdp', axis=0, tiled=True)  51.2 us
    all_gather x1, waiting for transfers between devices, on_device(): value_rows = lax.all_gather(value_local, 'fsdp', axis=0, tiled=True)  45.9 us
    all_gather x1, waiting for transfers between devices, on_device(): lax.all_gather(key_cols, 'fsdp', axis=0, tiled=True)  44.5 us
    all_gather x1, waiting for transfers between devices, on_device(): lax.all_gather(value_cols, 'fsdp', axis=0, tiled=True)  41.6 us
    all_gather x1, waiting for transfers between devices, on_device(): lax.all_gather(w_out, 'fsdp', axis=1, tiled=True)  41.2 us
  transfers between devices with their start and end apart: 9, of which 9 were waited for; matrix products, arithmetic and copies ran while one was open for 4% of the time, Pallas kernels for 0%

profile of v1, /device:TPU:1, one launch (start us, length us, event | category | flops | bytes accessed | tf_op | source)
XLA Modules:
  0.0 667.0 jit_solution(4176876372559982364)
XLA Ops:
  7.2 0.0 copy-start
  7.2 0.0 all-gather.9.cloned.1.call-start
  7.3 0.7 copy-done
  8.0 0.6 constant_dynamic-slice_fusion.1
  8.6 0.0 all-gather.9.cloned.1.call-update
  8.7 0.0 all-gather.15.cloned.1.call-start
  8.7 1.4 constant_dynamic-slice_fusion
  10.1 0.0 all-gather.15.cloned.1.call-update
  10.1 0.0 all-gather.13.cloned.1.call-start
  10.2 0.7 all-gather.13.cloned.1.call-update
  10.8 0.0 all-gather.11.cloned.1.call-start
  10.9 2.1 fusion.27
  13.0 44.5 %all-gather.9.cloned.1.call-done = bf16[4096,128]{1,0:T(8,128)(2,1)} async-done(((bf16[128,128]{1,0:T(8,128)(2,1)}), bf16[4096,128]{1,0:T(8,128)(2,1)}) %all-gather.9.cloned.1.call-update) | async-done | bytes 1048592 | tf_op jit(solution)/shard_map/all_gather | solution.py:71
  57.5 3.3 convolution_convert_fusion.6
  60.8 0.0 all-gather.11.cloned.1.call-update
  60.8 0.0 all-gather.17.cloned.1.call-start
  60.9 41.6 %all-gather.15.cloned.1.call-done = bf16[4096,128]{1,0:T(8,128)(2,1)} async-done(((bf16[128,128]{1,0:T(8,128)(2,1)}), bf16[4096,128]{1,0:T(8,128)(2,1)}) %all-gather.15.cloned.1.call-update) | async-done | bytes 1048592 | tf_op jit(solution)/shard_map/all_gather | solution.py:76
  102.4 2.7 convolution_convert_fusion.5
  105.1 0.0 all-gather.17.cloned.1.call-update
  105.1 0.0 all-gather.19.cloned.1.call-start
  105.2 0.5 all-gather.19.cloned.1.call-update
  105.7 0.0 all-gather.21.cloned.1.call-start
  105.8 51.2 %all-gather.13.cloned.1.call-done = bf16[4096,1024]{1,0:T(8,128)(2,1)} async-done(((bf16[128,1024]{1,0:T(8,128)(2,1)}), bf16[4096,1024]{1,0:T(8,128)(2,1)}) %all-gather.13.cloned.1.call-update) | async-done | bytes 8388624 | tf_op jit(solution)/shard_map/all_gather | solution.py:66
  157.0 5.7 fusion.36
  162.7 0.1 copy.28
  162.8 40.4 %all-gather.11.cloned.1.call-done = bf16[8192,128]{1,0:T(8,128)(2,1)} async-done(((bf16[256,128]{1,0:T(8,128)(2,1)}), bf16[8192,128]{1,0:T(8,128)(2,1)}) %all-gather.11.cloned.1.call-update) | async-done | bytes 2097168 | tf_op jit(solution)/shard_map/all_gather | solution.py:91
  203.2 45.9 %all-gather.17.cloned.1.call-done = bf16[8192,128]{1,0:T(8,128)(2,1)} async-done(((bf16[256,128]{1,0:T(8,128)(2,1)}), bf16[8192,128]{1,0:T(8,128)(2,1)}) %all-gather.17.cloned.1.call-update) | async-done | bytes 2097168 | tf_op jit(solution)/shard_map/all_gather | solution.py:92
  249.1 0.1 broadcast_in_dim.77
  249.2 19.2 %while.15 = (s32[]{:T(128)}, f32[256,8]{0,1:T(8,128)S(1)}, f32[256,8]{0,1:T(8,128)S(1)}, f32[256,8,128]{2,0,1:T(8,128)S(1)}, s32[8]{0:T(128)S(1)}, /*index=5*/s3...) while((s32[]{:T(128)}, f32[256,8]{0,1:T(8,128)S(1)}, ...), condition=%wide.region_6.7_spmd.clone, body=%wide.region_1.6_spmd.clone.sunk | while | flops 1101796608 | bytes 29503820 | solution.py:111
  249.2 0.6 dynamic_slice.49
  250.5 8.7 %conditional.3 = ((f32[256,8]{0,1:T(8,128)S(1)}, f32[256,8]{0,1:T(8,128)S(1)}, f32[256,8,128]{2,0,1:T(8,128)S(1)})) conditional(s32[]{:T(128)} %convert_element_type.174, (f32[256,8]{0,1:T(8,128)S(1)}, f32[256,8]{0,1:T(8,128)S(1)}, f32[256,8,128]{2,0,1:T(8,128)S(1)}) %tuple.52, (s32[]{:T(128)}, s32[]{:T(128)}, bf16[8192,128]{1,0:T(8,128)(2,1)}, ...), branch_computations={%region_2.2_spmd, %region_3.5_spmd} | conditional | flops 1101796608 | bytes 29502546 | solution.py:101
  250.5 0.2 broadcast_compare_fusion
  250.7 2.4 fusion.2
  253.2 2.0 fusion.4
  255.2 3.9 fusion.8
  259.2 0.6 dynamic_slice.49
  260.5 0.6 dynamic_slice.49
  261.8 0.6 dynamic_slice.49
  263.1 0.6 dynamic_slice.49
  264.4 0.6 dynamic_slice.49
  265.7 0.6 dynamic_slice.49
  267.0 0.6 dynamic_slice.49
  268.4 0.3 copy.24
  268.8 0.1 divide_convert_fusion
  268.9 41.2 %all-gather.19.cloned.1.call-done = bf16[1024,4096]{1,0:T(8,128)(2,1)} async-done(((bf16[1024,128]{1,0:T(8,128)(2,1)}), bf16[1024,4096]{1,0:T(8,128)(2,1)}) %all-gather.19.cloned.1.call-update) | async-done | bytes 8388624 | tf_op jit(solution)/shard_map/all_gather | solution.py:116
  310.1 7.1 %convolution_convert_fusion.2 = bf16[256,4096]{1,0:T(8,128)(2,1)} fusion(bf16[256,1024]{0,1:T(8,128)(2,1)S(1)} %bitcast.57, bf16[1024,4096]{1,0:T(8,128)(2,1)} %all-gather.19.cloned.1.call-done), kind=kOutput, calls=%fused_computation.34 | convolution fusion | flops 2148532224 | bytes 11010048 | tf_op jit(solution)/shard_map/dot_general | solution.py:114
  317.2 0.0 all-gather.21.cloned.1.call-update
  317.3 0.1 compare_reduce_fusion
  317.4 0.5 convolution_compare_fusion
  317.9 100.7 %all-gather.21.cloned.1.call-done = bf16[1024,4096]{1,0:T(8,128)(2,1)} async-done(((bf16[256,4096]{1,0:T(8,128)(2,1)}), bf16[1024,4096]{1,0:T(8,128)(2,1)}) %all-gather.21.cloned.1.call-update) | async-done | bytes 8388624 | tf_op jit(solution)/shard_map/all_gather | solution.py:120
  418.6 6.9 %reduce_sum.55 = bf16[256,4096]{1,0:T(8,128)(2,1)} reduce(bf16[4,256,4096]{2,1,0:T(8,128)(2,1)} %bitcast.54, bf16[]{:T(256)} %constant.115.clone.1), dimensions={0}, to_apply=%region_7.8 | reduce | flops 3145728 | bytes 10485762 | tf_op jit(solution)/shard_map/reduce_sum | solution.py:119
  425.4 3.2 fusion.24
  428.7 2.0 convolution_convert_fusion
  430.7 80.9 %all_to_all.10 = bf16[32,24,4096]{2,1,0:T(8,128)(2,1)S(1)} all-to-all(bf16[32,24,4096]{2,1,0:T(8,128)(2,1)S(1)} %bitcast.52), channel_id=1, replica_groups=mesh['grp'=4,'fsdp'=32] {'fsdp'}, dimensions={0} | all-to-all | bytes 12582912 | tf_op jit(solution)/shard_map/all_to_all | solution.py:151
  511.5 11.7 %fusion.21 = f32[768,1536]{1,0:T(8,128)} fusion(bf16[768,4096]{1,0:T(8,128)(2,1)S(1)} %bitcast.56, bf16[1,4096,1536]{2,1,0:T(8,128)(2,1)S(1)} %bitcast.59), kind=kOutput, calls=%fused_computation.24 | convolution fusion | flops 9663676416 | bytes 23592960 | tf_op jit(solution)/shard_map/dot_general | solution.py:154
  523.2 10.4 %convolution_convert_fusion.1 = bf16[768,4096]{1,0:T(8,128)(2,1)} fusion(bf16[1,768,4096]{2,1,0:T(8,128)(2,1)} %param.25, f32[768,1536]{1,0:T(8,128)} %fusion.21), kind=kOutput, calls=%fused_computation.27 | convolution fusion | flops 4838522880 | bytes 17301504 | tf_op jit(solution)/shard_map/dot_general | solution.py:156
  533.6 4.8 all-to-all-start.1
  538.4 0.0 reduce-scatter.2.cloned.1.call-start
  538.4 0.1 fusion.41
  538.5 77.7 %all-to-all-done.1 = bf16[32,24,4096]{2,1,0:T(8,128)(2,1)} async-done(((bf16[32,24,4096]{2,1,0:T(8,128)(2,1)}), bf16[32,24,4096]{2,1,0:T(8,128)(2,1)}, u32[]{:S(2)}, u32[]{:S(2)}) %all-to-all-start.1) | async-done | bytes 6291488 | tf_op jit(solution)/shard_map/all_to_all | solution.py:157
  616.2 6.1 convolution_convert_fusion.3
  622.4 0.0 reduce-scatter.2.cloned.1.call-update
  622.4 35.7 %reduce-scatter.2.cloned.1.call-done = bf16[256,1024]{1,0:T(8,128)(2,1)} async-done(((bf16[256,4096]{1,0:T(8,128)(2,1)}), bf16[256,1024]{1,0:T(8,128)(2,1)}) %reduce-scatter.2.cloned.1.call-update) | async-done | bytes 524304 | tf_op jit(solution)/shard_map/reduce_scatter | solution.py:172
  658.1 2.0 add_convert_fusion
  (46 shorter events, 0.2 us)
Async XLA Ops:
  7.2 0.8 copy-start
  7.2 95.3 %copy-start.2 = (bf16[256,4096]{1,0:T(8,128)(2,1)S(1)}, bf16[256,4096]{1,0:T(8,128)(2,1)}, u32[]{:S(2)}) copy-start(bf16[256,4096]{1,0:T(8,128)(2,1)} %param.15) | copy-start | bytes 6291460
  7.2 95.3 %copy-start.6 = (f32[4096]{0:T(1024)S(1)}, f32[4096]{0:T(1024)}, u32[]{:S(2)}) copy-start(f32[4096]{0:T(1024)} %param.16) | copy-start | bytes 49156
  7.2 50.3 %all-gather.9.cloned.1.call-start = ((), (), s32[]{:S(2)}) async-start(), calls=%async_computation.3 | async-start | bytes 1081344 | tf_op jit(solution)/shard_map/all_gather | solution.py:71
  8.7 93.8 %all-gather.15.cloned.1.call-start = ((), (), s32[]{:S(2)}) async-start(), calls=%async_computation.6 | async-start | bytes 1081344 | tf_op jit(solution)/shard_map/all_gather | solution.py:76
  10.1 146.8 %all-gather.13.cloned.1.call-start = ((), (), s32[]{:S(2)}) async-start(), calls=%async_computation.5 | async-start | bytes 8650752 | tf_op jit(solution)/shard_map/all_gather | solution.py:66
  10.8 192.3 %all-gather.11.cloned.1.call-start = ((), (), s32[]{:S(2)}) async-start(), calls=%async_computation.4 | async-start | bytes 2162688 | tf_op jit(solution)/shard_map/all_gather | solution.py:91
  60.8 188.3 %all-gather.17.cloned.1.call-start = ((), (), s32[]{:S(2)}) async-start(), calls=%async_computation.7 | async-start | bytes 2162688 | tf_op jit(solution)/shard_map/all_gather | solution.py:92
  105.1 205.0 %all-gather.19.cloned.1.call-start = ((), (), s32[]{:S(2)}) async-start(), calls=%async_computation.8 | async-start | bytes 8650752 | tf_op jit(solution)/shard_map/all_gather | solution.py:116
  105.7 312.8 %all-gather.21.cloned.1.call-start = ((), (), s32[]{:S(2)}) async-start(), calls=%async_computation.10 | async-start | bytes 10485760 | tf_op jit(solution)/shard_map/all_gather | solution.py:120
  310.1 7.2 %copy-start.3 = (s32[256,8]{0,1:T(8,128)S(1)}, s32[256,8]{0,1:T(8,128)}, u32[]{:S(2)}) copy-start(s32[256,8]{0,1:T(8,128)} %param.22) | copy-start | bytes 24580
  425.4 3.2 copy-start.4
  428.7 82.9 %slice-start = ((s8[12582912]{0:T(1024)(128)(4,1)}), s8[4194304]{0:T(1024)(128)(4,1)S(1)}, s32[]{:S(2)}) async-start(s8[12582912]{0:T(1024)(128)(4,1)} %bitcast.58), calls=%async_computation.11 | async-start | bytes 8388608
  428.7 82.9 %slice-start.1 = ((s8[12582912]{0:T(1024)(128)(4,1)}), s8[4194304]{0:T(1024)(128)(4,1)S(1)}, s32[]{:S(2)}) async-start(s8[12582912]{0:T(1024)(128)(4,1)} %bitcast.58), calls=%async_computation.12 | async-start | bytes 8388608
  430.7 80.9 %slice-start.2 = ((s8[12582912]{0:T(1024)(128)(4,1)}), s8[4194304]{0:T(1024)(128)(4,1)S(1)}, s32[]{:S(2)}) async-start(s8[12582912]{0:T(1024)(128)(4,1)} %bitcast.58), calls=%async_computation.13 | async-start | bytes 8388608
  533.6 4.9 copy-start.5
  533.6 82.7 %all-to-all-start.1 = ((bf16[32,24,4096]{2,1,0:T(8,128)(2,1)}), bf16[32,24,4096]{2,1,0:T(8,128)(2,1)}, u32[]{:S(2)}, u32[]{:S(2)}) async-start(bf16[32,24,4096]{2,1,0:T(8,128)(2,1)} %bitcast.55), calls=%async_computation.1 | async-start | bytes 12582912 | tf_op jit(solution)/shard_map/all_to_all | solution.py:157
  538.4 119.7 %reduce-scatter.2.cloned.1.call-start = ((), (), s32[]{:S(2)}) async-start(), calls=%async_computation.9 | async-start | bytes 2621440 | tf_op jit(solution)/shard_map/reduce_scatter | solution.py:172
  616.2 43.9 %copy-start.1 = (bf16[128,256]{1,0:T(8,128)(2,1)S(1)}, bf16[128,256]{1,0:T(8,128)(2,1)}, u32[]{:S(2)}) copy-start(bf16[128,256]{1,0:T(8,128)(2,1)} %param.19) | copy-start | bytes 196612
Sparse Core Ops, SparseCore 0:
  10.9 46.5 all-gather.8
  60.3 42.0 all-gather.14
  104.7 52.1 all-gather.12
  159.6 43.4 all-gather.10
  205.9 43.2 all-gather.16
  251.2 58.9 all-gather.18
  317.4 101.1 all-gather.20
  622.5 35.5 reduce-scatter.1
